TPU v7x, 1024 devices: a whole 4x4x32 slice. The times are simulated.
1024 devices in a mesh: dp: 64 (over z, core), expert: 16 (over x, y).
Axes of the slice: x: 4, y: 4, z: 32, core: 2. Of those that a mesh axis runs over, the one named last changes fastest.
Arguments:
- tokens: bfloat16 [8192, 2048], P('dp', 'expert'), may hold values from -6 to 6
- routes: int32 [8192, 4], P('dp'), may hold values from 0 to 63, all different within a row; in each aligned block of 128 rows (0 to 127, 128 to 255, ...) at most 10 rows name the same one
- gate_weights: float32 [8192, 4], P('dp'), may hold values from 0.1 to 1
- gate_up_weight: bfloat16 [64, 2048, 2, 2816], P('dp', None, None, 'expert'), may hold values from -0.125 to 0.125
- down_weight: bfloat16 [64, 2816, 2048], P('dp', 'expert'), may hold values from -0.109375 to 0.109375
Outputs:
- combined: bfloat16 [8192, 2048], P('dp', 'expert')
Inputs may be any that keep to these rules, and one draw needn't show every extreme that they name: `routes`: each row names 4 different experts. Within the 128 rows of one dp shard no expert is named more than 10 times, and in every draw some expert is named exactly 10 times within some shard.
All inputs are finite; a program needn't handle non-finite values.
Results may differ from a plain program's by a relative error of at most 0.015.
Values may be sent and summed in bfloat16 or wider, within the bound.
A program may use at most 32 MiB of HBM per device.

v0:
```python
from functools import partial

import jax
import jax.numpy as jnp
from jax import lax
from jax.sharding import PartitionSpec as P


def slot_numbers(assigned, count):
    onehot = (assigned[:, None] == jnp.arange(count, dtype=jnp.int32)[None, :]).astype(jnp.int32)
    earlier = jnp.cumsum(onehot, axis=0) - onehot
    return jnp.sum(earlier * onehot, axis=1)


def add_rows(gate_up, total, portion, offset):
    return jnp.dot(portion, gate_up, preferred_element_type=jnp.float32)


def activate(total, width_dev):
    gate_part = total[:, :width_dev]
    up_part = total[:, width_dev:]
    return (jax.nn.silu(gate_part) * up_part).astype(jnp.bfloat16)


def per_device(tokens, routes, gate_weights, gate_up_weight, down_weight):
    tok_rows = tokens.shape[0]
    feature_cols = tokens.shape[1]
    groups = lax.axis_size("dp")
    capacity = 5 * tok_rows // groups
    assigned = routes.reshape(-1)
    slot_index = slot_numbers(assigned, groups)
    dest_index = assigned * capacity + slot_index
    copies = jnp.repeat(tokens, routes.shape[1], axis=0)
    outgoing = jnp.zeros((groups * capacity, feature_cols), jnp.bfloat16).at[dest_index].set(copies)
    incoming = lax.all_to_all(
        outgoing.reshape(groups, capacity, feature_cols),
        "dp",
        split_axis=0,
        concat_axis=0,
        tiled=True,
    )
    width_dev = down_weight.shape[1]
    model_width = down_weight.shape[2]
    gate_up = gate_up_weight.reshape(model_width, 2 * width_dev)
    down_rows = down_weight.reshape(width_dev, model_width)
    fold_rows = partial(add_rows, gate_up)
    row_block = incoming.reshape(-1, feature_cols)
    empty = jnp.zeros((row_block.shape[0], 2 * width_dev), jnp.float32)
    total = fold_rows(empty, lax.all_gather(row_block, "expert", axis=1, tiled=True), jnp.int32(0))
    partial_sum = jnp.dot(activate(total, width_dev), down_rows, preferred_element_type=jnp.float32)
    partial_sum = partial_sum.reshape(groups, capacity, model_width)
    summed = lax.psum_scatter(
        partial_sum.astype(jnp.bfloat16), "expert", scatter_dimension=2, tiled=True
    )
    returned = lax.all_to_all(summed, "dp", split_axis=0, concat_axis=0, tiled=True)
    lookup = returned.reshape(groups * capacity, feature_cols)
    picked = lookup[dest_index].reshape(tok_rows, routes.shape[1], feature_cols).astype(jnp.float32)
    return jnp.sum(gate_weights[:, :, None] * picked, axis=1).astype(jnp.bfloat16)


def solution(mesh):
    return jax.shard_map(
        per_device,
        mesh=mesh,
        in_specs=(
            P("dp", "expert"),
            P("dp", None),
            P("dp", None),
            P("dp", None, None, "expert"),
            P("dp", "expert", None),
        ),
        out_specs=P("dp", "expert"),
        check_vma=False,
    )
```

profile of v0, /device:TPU:1, one launch (start us, length us, event | category | flops | bytes accessed | tf_op | source)
XLA Modules:
  0.0 369.1 jit_solution(17772531237782133583)
XLA Ops:
  6.5 0.0 copy-start
  6.5 0.0 all-gather.2.cloned.1.call-start
  6.5 0.9 copy.18
  7.4 0.1 eq.29
  7.5 0.1 eq.25
  7.7 0.7 broadcast_multiply_fusion
  8.4 1.2 reduce-window.6
  9.6 0.2 slice_reduce_fusion
  9.8 0.1 copy.17
  10.0 0.1 mul.37
  10.1 0.1 fusion.6
  10.2 0.8 broadcast_in_dim.5
  11.0 1.8 scatter_custom_fusion
  12.8 0.1 reshape.72
  12.9 71.5 %all_to_all.10 = bf16[64,10,128]{2,1,0:T(8,128)(2,1)S(1)} all-to-all(bf16[64,10,128]{2,1,0:T(8,128)(2,1)S(1)} %reshape.72), channel_id=1, replica_groups=mesh['dp'=64,'expert'=16] {'dp'}, dimensions={0} | all-to-all | bytes 327680 | tf_op jit(solution)/shard_map/all_to_all | solution.py:35
  84.4 0.7 reshape.73
  85.1 0.0 all-gather.2.cloned.1.call-update
  85.1 0.0 reduce-scatter.4.cloned.1.call-start
  85.2 68.0 %all-gather.2.cloned.1.call-done = bf16[640,2048]{1,0:T(8,128)(2,1)} async-done(((bf16[640,128]{1,0:T(8,128)(2,1)}), bf16[640,2048]{1,0:T(8,128)(2,1)}) %all-gather.2.cloned.1.call-update) | async-done | bytes 2621456 | tf_op jit(solution)/shard_map/all_gather | solution.py:49
  153.1 0.0 copy-done
  153.2 3.1 fusion.10
  156.2 0.0 copy-start.1
  156.2 0.1 fusion.1
  156.4 0.2 copy.21
  156.6 0.1 dot_general.9
  156.7 0.6 copy-done.1
  157.3 2.4 convolution_convert_fusion
  159.8 10.2 %copy.24 = bf16[64,10,2048]{0,1,2:T(8,128)(2,1)} copy(bf16[64,10,2048]{2,0,1:T(8,128)(2,1)} %convolution_convert_fusion) | data formatting | bytes 5242880
  169.9 10.6 %reshape.95 = bf16[2048,640]{1,0:T(8,128)(2,1)} reshape(bf16[2048,10,64]{2,1,0:T(8,128)(2,1)} %bitcast.35) | data formatting | bytes 5242880
  180.5 0.0 copy-start.2
  180.5 0.0 reduce-scatter.4.cloned.1.call-update
  180.6 110.1 %reduce-scatter.4.cloned.1.call-done = bf16[128,640]{1,0:T(8,128)(2,1)} async-done(((bf16[2048,640]{1,0:T(8,128)(2,1)}), bf16[128,640]{1,0:T(8,128)(2,1)}) %reduce-scatter.4.cloned.1.call-update) | async-done | bytes 163856
  290.6 1.2 reshape.96
  291.9 1.3 copy.23
  293.1 25.5 %all-to-all-start.1 = ((bf16[64,10,128]{2,1,0:T(8,128)(2,1)}), bf16[64,10,128]{2,1,0:T(8,128)(2,1)S(1)}, u32[]{:S(2)}, u32[]{:S(2)}) async-start(bf16[64,10,128]{2,1,0:T(8,128)(2,1)} %copy.23), calls=%async_computation.1 | async-start | bytes 524288 | tf_op jit(solution)/shard_map/all_to_all | solution.py:55
  318.6 0.0 copy-done.2
  318.7 0.1 copy.16
  318.8 41.2 %all-to-all-done.1 = bf16[64,10,128]{2,1,0:T(8,128)(2,1)S(1)} async-done(((bf16[64,10,128]{2,1,0:T(8,128)(2,1)}), bf16[64,10,128]{2,1,0:T(8,128)(2,1)S(1)}, u32[]{:S(2)}, u32[]{:S(2)}) %all-to-all-start.1) | async-done | bytes 163872 | tf_op jit(solution)/shard_map/all_to_all | solution.py:55
  359.9 0.1 reshape.76
  360.0 1.3 gather_fusion
  361.4 0.9 fusion.3
  (5 shorter events, 0.1 us)
Async XLA Ops:
  6.5 146.6 %copy-start = (bf16[1,2048,2,176]{1,3,2,0:T(8,128)(2,1)S(1)}, bf16[1,2048,2,176]{1,3,2,0:T(8,128)(2,1)}, u32[]{:S(2)}) copy-start(bf16[1,2048,2,176]{1,3,2,0:T(8,128)(2,1)} %param.8) | copy-start | bytes 4325380
  6.5 146.6 %all-gather.2.cloned.1.call-start = ((), (), s32[]{:S(2)}) async-start(), calls=%async_computation.3 | async-start | bytes 2785280 | tf_op jit(solution)/shard_map/all_gather | solution.py:49
  85.1 205.5 %reduce-scatter.4.cloned.1.call-start = ((), (), s32[]{:S(2)}) async-start(), calls=%async_computation.4 | async-start | bytes 2785280
  156.2 1.1 copy-start.1
  180.5 138.1 %copy-start.2 = (f32[128,4]{0,1:T(4,128)S(1)}, f32[128,4]{0,1:T(4,128)}, u32[]{:S(2)}) copy-start(f32[128,4]{0,1:T(4,128)} %param.7) | copy-start | bytes 6148
  293.1 66.8 %all-to-all-start.1 = ((bf16[64,10,128]{2,1,0:T(8,128)(2,1)}), bf16[64,10,128]{2,1,0:T(8,128)(2,1)S(1)}, u32[]{:S(2)}, u32[]{:S(2)}) async-start(bf16[64,10,128]{2,1,0:T(8,128)(2,1)} %copy.23), calls=%async_computation.1 | async-start | bytes 524288 | tf_op jit(solution)/shard_map/all_to_all | solution.py:55
Sparse Core Ops, SparseCore 0:
  85.2 67.8 all-gather.1
  180.7 109.8 reduce-scatter.3
where the time goes:
time: 370 us; the launch traced here: 369 us
  waiting for transfers between devices  219 us (59%)
  blocking collectives  71.5 us (19%)
  local copies, waits for them, and re-layouts  30.7 us (8%)
  starting transfers between devices  25.6 us (7%)
  between operations  13.5 us (4%)
  matrix products  5.48 us (1%)
    unnamed x3, waiting for transfers between devices  110 us
    all_to_all x1, blocking collectives, per_device(): lax.all_to_all(outgoing.reshape(groups, capacity, feature_cols), 'dp', sp...  71.5 us
    all_gather x1, waiting for transfers between devices, per_device(): lax.all_gather(row_block, 'expert', axis=1, tiled=True)  68 us
    all_to_all x1, waiting for transfers between devices, per_device(): lax.all_to_all(summed, 'dp', split_axis=0, concat_axis=0, tiled=True)  41.2 us
    all_to_all x1, starting transfers between devices, per_device(): lax.all_to_all(summed, 'dp', split_axis=0, concat_axis=0, tiled=True)  25.5 us
    unnamed x11, local copies, waits for them, and re-layouts  23.7 us
  transfers between devices with their start and end apart: 3, of which 3 were waited for; matrix products, arithmetic and copies ran while one was open for 0% of the time, Pallas kernels for 0%

commit v1 on v0

v1 whole, which is shorter than its diff:
```python
import functools
import math

import jax
import jax.numpy as jnp
from jax import lax
from jax.experimental import pallas as pl
from jax.experimental.pallas import tpu as pltpu
from jax.sharding import PartitionSpec as P

BLOCKS = 4
MESH_ID = pl.DeviceIdType.MESH
F32 = jnp.float32
BF16 = jnp.bfloat16


def offset_of(i, n):
    m = i // 2
    dist = jnp.where(m < n // 4, 2 * m, n - 1 - 2 * m)
    back = jnp.where(m == 0, n // 2, n - dist)
    return jnp.where(i % 2 == 0, dist, back)


def position_of(r, n):
    dist = jnp.where(r == n // 2, 0, jnp.minimum(r, n - r))
    m = jnp.where(dist % 2 == 0, dist // 2, (n - 1 - dist) // 2)
    return 2 * m + jnp.where(r >= n // 2, 1, 0)


def kernel(
    n, side, cap, blocks,
    tokens, routes, gates, gate_up_hbm, down_hbm, out,
    gate_up, down, outgoing, incoming, gathered, part, landed, sums, landed2, results, returned,
    load_sem, own_sem, z1_send, z1_recv, ag_send, ag_recv1, ag_recv2, rs1_send, rs1_recv, rs2_send, rs2_recv,
    z2_send, z2_recv,
):
    d = lax.axis_index("dp")
    j = lax.axis_index("expert")
    coords = (j // side, j % side)
    tok, feat = tokens.shape
    rows = n * cap
    half = cap // 2
    block_rows = rows // blocks
    per_block = n // blocks
    width = gate_up.shape[1]

    def group(c0, c1):
        return c0 * side + c1

    def peer(axis, o):
        moved = lax.rem(coords[axis] + o, side)
        return group(moved, coords[1]) if axis == 0 else group(coords[0], moved)

    loads = [
        pltpu.make_async_copy(gate_up_hbm, gate_up, load_sem.at[0]),
        pltpu.make_async_copy(down_hbm, down, load_sem.at[1]),
    ]
    for load in loads:
        load.start()

    barrier = pltpu.get_barrier_semaphore()

    def greet(i, carry):
        pl.semaphore_signal(barrier, inc=1, device_id=(lax.rem(d + i, n), j), device_id_type=MESH_ID)
        return carry

    lax.fori_loop(1, n, greet, 0)
    for axis in range(2):
        for o in range(1, side):
            pl.semaphore_signal(barrier, inc=1, device_id=(d, peer(axis, o)), device_id_type=MESH_ID)

    expert_iota = lax.broadcasted_iota(jnp.int32, (n, tok), 0)
    names = [routes[k : k + 1, :] for k in range(routes.shape[0])]
    hits = [expert_iota == name for name in names]
    chosen = functools.reduce(jnp.logical_or, hits).astype(F32).astype(BF16)
    before = (
        lax.broadcasted_iota(jnp.int32, (tok, tok), 0) < lax.broadcasted_iota(jnp.int32, (tok, tok), 1)
    ).astype(F32).astype(BF16)
    earlier = jnp.dot(chosen, before, preferred_element_type=F32)
    row_iota = lax.broadcasted_iota(jnp.int32, (rows, tok), 0)
    picks = []
    for k, name in enumerate(names):
        slot = jnp.sum(jnp.where(hits[k], earlier, 0.0), axis=0, keepdims=True).astype(jnp.int32)
        r = lax.rem(d - name + n, n)
        picks.append(row_iota == position_of(r, n) * cap + slot)
    dispatch = functools.reduce(jnp.logical_or, picks).astype(F32).astype(BF16)
    sent = jnp.dot(dispatch, tokens[...], preferred_element_type=F32).astype(BF16)
    outgoing[...] = sent.reshape(rows // 2, 2, feat)

    pl.semaphore_wait(barrier, n - 1 + 2 * (side - 1))

    def chunk(ref, i):
        return ref.at[pl.ds(i * half, half)]

    own = pltpu.make_async_copy(chunk(outgoing, 0), chunk(incoming, 0), own_sem)
    own.start()

    def send1(i, carry):
        to = lax.rem(d - offset_of(i, n) + n, n)
        pltpu.make_async_remote_copy(
            chunk(outgoing, i), chunk(incoming, i), z1_send, z1_recv.at[i // per_block],
            device_id=(to, j), device_id_type=MESH_ID,
        ).start()
        return carry

    lax.fori_loop(1, n, send1, 0)

    def await_bytes(ref, sem):
        pltpu.make_async_copy(ref, ref, sem).wait()

    def columns(c0, c1):
        return pl.ds(pl.multiple_of(group(c0, c1) * feat, feat), feat)

    def gather_send(b, cols, axis, o, sem):
        pltpu.make_async_remote_copy(
            gathered.at[b, :, cols], gathered.at[b, :, cols], ag_send, sem,
            device_id=(d, peer(axis, o)), device_id_type=MESH_ID,
        ).start()

    def axes_of(b):
        return (0, 1) if b % 2 == 0 else (1, 0)

    def stage1(b):
        first = cap // 2 if b == 0 else 0
        if b == 0:
            own.wait()
        lo = b * block_rows // 2
        await_bytes(incoming.at[pl.ds(lo + first, block_rows // 2 - first)], z1_recv.at[b])
        cols = columns(*coords)
        gathered[b, :, cols] = incoming[pl.ds(lo, block_rows // 2)].reshape(block_rows, feat)
        a1, a2 = axes_of(b)
        for o in range(1, side):
            gather_send(b, cols, a1, o, ag_recv1.at[b, o])
        for o in range(1, side):
            gather_send(b, cols, a2, o, ag_recv2.at[b])

    def stage2(b):
        a1, a2 = axes_of(b)
        for o in range(1, side):
            moved = lax.rem(coords[a1] + side - o, side)
            cols = columns(moved, coords[1]) if a1 == 0 else columns(coords[0], moved)
            await_bytes(gathered.at[b, :, cols], ag_recv1.at[b, o])
            for q in range(1, side):
                gather_send(b, cols, a2, q, ag_recv2.at[b])

    def stage3(b):
        await_bytes(gathered.at[b, :, pl.ds(0, feat * side * (side - 1))], ag_recv2.at[b])
        x = gathered[b]
        contract = (((1,), (1,)), ((), ()))
        gate = lax.dot_general(x, gate_up[0], contract, preferred_element_type=F32)
        up = lax.dot_general(x, gate_up[1], contract, preferred_element_type=F32)
        hidden = (gate / (1.0 + jnp.exp(-gate)) * up).astype(BF16)
        first = axes_of(b)[1]
        for c0 in range(side):
            wide = side * feat
            piece = jnp.dot(hidden, down[:, c0 * wide : (c0 + 1) * wide], preferred_element_type=F32).astype(BF16)
            if first == 0:
                part[b, c0] = piece
            else:
                for c1 in range(side):
                    part[b, c1, :, c0 * feat : (c0 + 1) * feat] = piece[:, c1 * feat : (c1 + 1) * feat]
        for o in range(1, side):
            pltpu.make_async_remote_copy(
                part.at[b, lax.rem(coords[first] + o, side)], landed.at[b, o - 1], rs1_send, rs1_recv.at[b],
                device_id=(d, peer(first, o)), device_id_type=MESH_ID,
            ).start()

    def stage4(b):
        second, first = axes_of(b)
        await_bytes(landed.at[b], rs1_recv.at[b])
        total = part[b, coords[first]].astype(F32)
        for o in range(1, side):
            total += landed[b, o - 1].astype(F32)
        for c in range(side):
            sums[b, c] = total[:, c * feat : (c + 1) * feat].astype(BF16)
        for o in range(1, side):
            pltpu.make_async_remote_copy(
                sums.at[b, lax.rem(coords[second] + o, side)], landed2.at[b, o - 1], rs2_send, rs2_recv.at[b],
                device_id=(d, peer(second, o)), device_id_type=MESH_ID,
            ).start()

    def send2(i, carry):
        to = lax.rem(d + offset_of(i, n), n)
        pltpu.make_async_remote_copy(
            chunk(results, i), chunk(returned, i), z2_send, z2_recv, device_id=(to, j), device_id_type=MESH_ID
        ).start()
        return carry

    def stage5(b):
        second = axes_of(b)[0]
        await_bytes(landed2.at[b], rs2_recv.at[b])
        total = sums[b, coords[second]].astype(F32)
        for o in range(1, side):
            total += landed2[b, o - 1].astype(F32)
        pairs = total.astype(BF16).reshape(block_rows // 2, 2, feat)
        results[pl.ds(b * block_rows // 2, block_rows // 2)] = pairs
        if b == 0:
            pltpu.make_async_copy(chunk(results, 0), chunk(returned, 0), own_sem).start()
        lax.fori_loop(max(1, b * per_block), (b + 1) * per_block, send2, 0)

    for t in range(blocks + 2):
        if t < blocks:
            stage1(t)
            stage2(t)
        if t >= 2:
            stage4(t - 2)
        if t == 1:
            for load in loads:
                load.wait()
        if 1 <= t < blocks + 1:
            stage3(t - 1)
        if t >= 2:
            stage5(t - 2)

    weight = jnp.zeros((rows, tok), F32)
    for k, pick in enumerate(picks):
        weight = jnp.where(pick, gates[k : k + 1, :], weight)

    pltpu.make_async_copy(chunk(results, 0), chunk(returned, 0), own_sem).wait()
    await_bytes(returned.at[pl.ds(half, rows // 2 - half)], z2_recv)
    back = returned[...].reshape(rows, feat)
    total = jnp.zeros((tok, feat), F32)
    for _ in range(3):
        term = weight.astype(BF16)
        weight = weight - term.astype(F32)
        total += lax.dot_general(term, back, (((0,), (0,)), ((), ())), preferred_element_type=F32)
    out[...] = total.astype(BF16)

    await_bytes(outgoing.at[pl.ds(half, rows // 2 - half)], z1_send)
    await_bytes(results.at[pl.ds(half, rows // 2 - half)], z2_send)
    await_bytes(gathered.at[:, :, pl.ds(0, feat * (side * side - 1))], ag_send)
    await_bytes(landed, rs1_send)
    await_bytes(landed2, rs2_send)


def per_device(n, side, blocks, tokens, routes, gate_weights, gate_up_weight, down_weight):
    tok, feat = tokens.shape
    cap = 5 * tok // 64
    rows = n * cap
    block_rows = rows // blocks
    _, model, _, width = gate_up_weight.shape
    gate_up = gate_up_weight.transpose(0, 2, 3, 1).reshape(2, width, model)
    down = down_weight.reshape(width, model)
    dma = pltpu.SemaphoreType.DMA
    vmem = pl.BlockSpec(memory_space=pltpu.VMEM)
    anywhere = pl.BlockSpec(memory_space=pl.ANY)
    return pl.pallas_call(
        functools.partial(kernel, n, side, cap, blocks),
        out_shape=jax.ShapeDtypeStruct((tok, feat), BF16),
        in_specs=[vmem, vmem, vmem, anywhere, anywhere],
        out_specs=vmem,
        scratch_shapes=[
            pltpu.VMEM((2, width, model), BF16),
            pltpu.VMEM((width, model), BF16),
            pltpu.VMEM((rows // 2, 2, feat), BF16),
            pltpu.VMEM((rows // 2, 2, feat), BF16),
            pltpu.VMEM((blocks, block_rows, model), BF16),
            pltpu.VMEM((blocks, side, block_rows, side * feat), BF16),
            pltpu.VMEM((blocks, side - 1, block_rows, side * feat), BF16),
            pltpu.VMEM((blocks, side, block_rows, feat), BF16),
            pltpu.VMEM((blocks, side - 1, block_rows, feat), BF16),
            pltpu.VMEM((rows // 2, 2, feat), BF16),
            pltpu.VMEM((rows // 2, 2, feat), BF16),
            dma((2,)),
            dma,
            dma,
            dma((blocks,)),
            dma,
            dma((blocks, side)),
            dma((blocks,)),
            dma,
            dma((blocks,)),
            dma,
            dma((blocks,)),
            dma,
            dma,
        ],
        compiler_params=pltpu.CompilerParams(
            collective_id=0, has_side_effects=True, vmem_limit_bytes=48 * 1024 * 1024
        ),
        cost_estimate=pl.CostEstimate(
            flops=6 * rows * model * width, bytes_accessed=6 * width * model, transcendentals=rows * width
        ),
    )(tokens, routes.T, gate_weights.T, gate_up, down)


def solution(mesh):
    n = mesh.shape["dp"]
    side = math.isqrt(mesh.shape["expert"])
    return jax.shard_map(
        functools.partial(per_device, n, side, BLOCKS),
        mesh=mesh,
        in_specs=(
            P("dp", "expert"),
            P("dp", None),
            P("dp", None),
            P("dp", None, None, "expert"),
            P("dp", "expert", None),
        ),
        out_specs=P("dp", "expert"),
        check_vma=False,
    )
```

time: 370 us -> 110 us (0.30)
  waiting for transfers between devices: 219 us -> 0 us
  Pallas kernels: 0 us -> 104 us
  blocking collectives: 71.5 us -> 0 us
  starting transfers between devices: 25.6 us -> 0 us
  local copies, waits for them, and re-layouts: 30.7 us -> 5.21 us
  between operations: 13.5 us -> 0.01 us
  matrix products: 5.48 us -> 0 us
    unnamed x3 -> x0, waiting for transfers between devices: 110 us -> none
    pallas_call x0 -> x1, Pallas kernels: none -> 104 us  [per_device(): pl.pallas_call(functools.partial(kernel, n, side, cap, blocks), out_shape...]
    all_to_all x1 -> x0, blocking collectives: 71.5 us -> none  [per_device(): lax.all_to_all(outgoing.reshape(groups, capacity, feature_cols), 'dp', sp...]
    all_gather x1 -> x0, waiting for transfers between devices: 68 us -> none  [per_device(): lax.all_gather(row_block, 'expert', axis=1, tiled=True)]
    all_to_all x1 -> x0, waiting for transfers between devices: 41.2 us -> none  [per_device(): lax.all_to_all(summed, 'dp', split_axis=0, concat_axis=0, tiled=True)]
    all_to_all x1 -> x0, starting transfers between devices: 25.5 us -> none  [per_device(): lax.all_to_all(summed, 'dp', split_axis=0, concat_axis=0, tiled=True)]
    unnamed x11, local copies, waits for them, and re-layouts: 23.7 us -> 5.21 us
    dot_general x2 -> x0, matrix products: 5.48 us -> none  [the longest x1 3.06 us: add_rows(): return jnp.dot(portion, gate_up, preferred_element_type=jnp.float32)]
  transfers between devices with their start and end apart: 3 -> 0, of which waited for: 3 -> 0; matrix products, arithmetic and copies ran while one was open for 0% -> 0% of each run, Pallas kernels for 0% -> 0%
where the time goes in v1:
time: 110 us; the launch traced here: 109 us
  Pallas kernels  104 us (95%)
  local copies, waits for them, and re-layouts  5.21 us (5%)
    pallas_call x1, Pallas kernels, per_device(): pl.pallas_call(functools.partial(kernel, n, side, cap, blocks), out_shape...  104 us
    unnamed x11, local copies, waits for them, and re-layouts  5.21 us

profile of v1, /device:TPU:1, one launch (start us, length us, event | category | flops | bytes accessed | tf_op | source)
XLA Modules:
  0.0 109.3 jit_solution(9695895706707795138)
XLA Ops:
  0.0 0.0 copy-start
  0.0 1.4 %copy-done = bf16[1,2048,2,176]{1,3,2,0:T(8,128)(2,1)S(1)} copy-done((bf16[1,2048,2,176]{1,3,2,0:T(8,128)(2,1)S(1)}, bf16[1,2048,2,176]{1,3,2,0:T(8,128)(2,1)}, u32[]{:S(2)}) %copy-start) | copy-done | bytes 1441816
  1.4 0.0 copy-start.1
  1.4 1.1 %copy-done.1 = bf16[1,176,2048]{2,1,0:T(8,128)(2,1)S(1)} copy-done((bf16[1,176,2048]{2,1,0:T(8,128)(2,1)S(1)}, bf16[1,176,2048]{2,1,0:T(8,128)(2,1)}, u32[]{:S(2)}) %copy-start.1) | copy-done | bytes 720920
  2.5 0.0 copy-start.2
  2.5 0.8 copy-done.2
  3.2 0.0 copy-start.3
  3.2 0.7 copy-done.3
  3.9 0.0 copy-start.4
  3.9 0.7 copy-done.4
  4.6 104.0 %shard_map.55 = bf16[128,128]{1,0:T(8,128)(2,1)S(1)} custom-call(bf16[128,128]{1,0:T(8,128)(2,1)S(1)} %copy-done.2, s32[4,128]{1,0:T(4,128)S(1)} %bitcast.8, f32[4,128]{1,0:T(4,128)S(1)} %bitcast.9, bf16[2,176,2048]{2,1,0:T(8,128)(2,1)S(1)} %bitcast.6, bf16[176,2048]{1,0:T(8,128)(2,1)S(1)} %bitcast.7), custom_call_target="tpu_custom_call" | custom-call | flops 1384120320 | bytes 2162688 | tf_op jit(solution)/shard_map/pallas_call | solution.py:247
  108.6 0.6 copy.7
Async XLA Ops:
  0.0 1.4 %copy-start = (bf16[1,2048,2,176]{1,3,2,0:T(8,128)(2,1)S(1)}, bf16[1,2048,2,176]{1,3,2,0:T(8,128)(2,1)}, u32[]{:S(2)}) copy-start(bf16[1,2048,2,176]{1,3,2,0:T(8,128)(2,1)} %param.8) | copy-start | bytes 4325380
  1.4 1.1 %copy-start.1 = (bf16[1,176,2048]{2,1,0:T(8,128)(2,1)S(1)}, bf16[1,176,2048]{2,1,0:T(8,128)(2,1)}, u32[]{:S(2)}) copy-start(bf16[1,176,2048]{2,1,0:T(8,128)(2,1)} %param.9) | copy-start | bytes 2162692
  2.5 0.8 copy-start.2
  3.2 0.7 copy-start.3
  3.9 0.7 copy-start.4

commit v2 on v1

v2 whole, which is shorter than its diff:
```python
import functools
import math

import jax
import jax.numpy as jnp
from jax import lax
from jax.experimental import pallas as pl
from jax.experimental.pallas import tpu as pltpu
from jax.sharding import PartitionSpec as P

BLOCKS = 8
PERIOD = 1
MESH_ID = pl.DeviceIdType.MESH
F32 = jnp.float32
BF16 = jnp.bfloat16


def offset_of(i, n):
    back = jnp.where(i == 0, 0, n // 2 + i // 2)
    return jnp.where(i % 2 == 0, back, (n + 1 - i) // 2)


def position_of(r, n):
    near = jnp.where(r == 0, 0, n + 1 - 2 * r)
    return jnp.where(r > n // 2, 2 * r - n, near)


def kernel(
    n, side, cap, blocks, period,
    tokens_hbm, routes_hbm, gates_hbm, gate_up_hbm, down_hbm, out,
    tokens, routes, gates, gate_up, down, terms,
    outgoing, incoming, gathered, part, halves, wholes, sums, landed, results, returned,
    load_sem, own_sem, z1_send, z1_recv, light_send, light_recv, plane_send, plane_recv, half_send, half_recv,
    rhalf_send, rhalf_recv, rwhole_send, rwhole_recv, last_send, last_recv, z2_send, z2_recv,
):
    d = lax.axis_index("dp")
    j = lax.axis_index("expert")
    coords = (j // side, j % side)
    tok, feat = tokens.shape
    rows = n * cap
    half = cap // 2
    block_rows = rows // blocks
    per_block = n // blocks
    wide = side * feat
    mid = wide // 2

    def load(src, dst, i):
        copy = pltpu.make_async_copy(src, dst, load_sem.at[i])
        copy.start()
        return copy

    load_routes = load(routes_hbm, routes, 0)
    load_tokens = load(tokens_hbm, tokens, 1)
    load_gates = load(gates_hbm, gates, 2)
    weights = [load(gate_up_hbm, gate_up, 3), load(down_hbm, down, 4)]

    def peer(axis, o):
        moved = lax.rem(coords[axis] + side + o, side)
        return moved * side + coords[1] if axis == 0 else coords[0] * side + moved

    barrier = pltpu.get_barrier_semaphore()

    def greet(i, carry):
        pl.semaphore_signal(barrier, inc=1, device_id=(lax.rem(d + i, n), j), device_id_type=MESH_ID)
        return carry

    lax.fori_loop(1, n, greet, 0)
    for axis in range(2):
        for o in range(1, side):
            pl.semaphore_signal(barrier, inc=1, device_id=(d, peer(axis, o)), device_id_type=MESH_ID)

    load_routes.wait()
    expert_iota = lax.broadcasted_iota(jnp.int32, (n, tok), 0)
    names = [routes[k : k + 1, :] for k in range(routes.shape[0])]
    hits = [expert_iota == name for name in names]
    chosen = functools.reduce(jnp.logical_or, hits).astype(F32).astype(BF16)
    before = (
        lax.broadcasted_iota(jnp.int32, (tok, tok), 0) < lax.broadcasted_iota(jnp.int32, (tok, tok), 1)
    ).astype(F32).astype(BF16)
    earlier = jnp.dot(chosen, before, preferred_element_type=F32)
    row_iota = lax.broadcasted_iota(jnp.int32, (rows, tok), 0)
    picks = []
    for k, name in enumerate(names):
        slot = jnp.sum(jnp.where(hits[k], earlier, 0.0), axis=0, keepdims=True).astype(jnp.int32)
        r = lax.rem(d - name + n, n)
        picks.append(row_iota == position_of(r, n) * cap + slot)
    dispatch = functools.reduce(jnp.logical_or, picks).astype(F32).astype(BF16)
    load_tokens.wait()
    sent = jnp.dot(dispatch, tokens[...], preferred_element_type=F32).astype(BF16)
    outgoing[...] = sent.reshape(rows // 2, 2, feat)

    load_gates.wait()
    weight = jnp.zeros((rows, tok), F32)
    for k, pick in enumerate(picks):
        weight = jnp.where(pick, gates[k : k + 1, :], weight)
    for i in range(3):
        term = weight.astype(BF16)
        weight = weight - term.astype(F32)
        terms[i] = term

    pl.semaphore_wait(barrier, n - 1 + 2 * (side - 1))

    def chunk(ref, i):
        return ref.at[pl.ds(i * half, half)]

    def push(src, dst, send, recv, to):
        pltpu.make_async_remote_copy(
            src, dst, send, recv, device_id=to, device_id_type=MESH_ID
        ).start()

    def await_bytes(ref, sem):
        pltpu.make_async_copy(ref, ref, sem).wait()

    def send1(i, carry):
        to = (lax.rem(d - offset_of(i, n) + n, n), j)
        push(chunk(outgoing, i), chunk(incoming, i), z1_send, z1_recv.at[i // per_block], to)
        return carry

    def send2(i, carry):
        to = (lax.rem(d + offset_of(i, n), n), j)
        push(chunk(results, i), chunk(returned, i), z2_send, z2_recv, to)
        return carry

    own = pltpu.make_async_copy(chunk(outgoing, 0), chunk(incoming, 0), own_sem)
    own.start()
    lax.fori_loop(1, n, send1, 0)

    def lanes(c, width):
        return pl.ds(pl.multiple_of(c * width, width), width)

    def arrive(b):
        first, second = b % 2, 1 - b % 2
        skip = half if b == 0 else 0
        if b == 0:
            own.wait()
        lo = b * block_rows // 2
        await_bytes(incoming.at[pl.ds(lo + skip, block_rows // 2 - skip)], z1_recv.at[b])
        cols = lanes(coords[first], feat)
        gathered[b, coords[second], :, cols] = incoming[pl.ds(lo, block_rows // 2)].reshape(block_rows, feat)
        place = gathered.at[b, coords[second], :, cols]
        for o in range(1, side):
            push(place, place, light_send, light_recv.at[b], (d, peer(first, o)))

    def widen(b):
        second = 1 - b % 2
        place = gathered.at[b, coords[second]]
        await_bytes(place.at[:, pl.ds(0, wide - feat)], light_recv.at[b])
        for way, o in enumerate((1, -1)):
            push(place, place, plane_send, plane_recv.at[b, way], (d, peer(second, o)))

    def forward(b):
        second = 1 - b % 2
        for way, o in enumerate((1, -1)):
            strip = gathered.at[b, lax.rem(coords[second] + side - o, side)]
            await_bytes(strip, plane_recv.at[b, way])
            place = strip.at[:, pl.ds(way * mid, mid)]
            push(place, place, half_send, half_recv.at[b, way], (d, peer(second, o)))

    def experts(pair):
        b0, b1 = 2 * pair, 2 * pair + 1
        for b in (b0, b1):
            across = gathered.at[b, lax.rem(coords[1 - b % 2] + 2, side)]
            for way in range(2):
                await_bytes(across.at[:, pl.ds(way * mid, mid)], half_recv.at[b, way])
        contract = (((1,), (1,)), ((), ()))
        gate = up = 0.0
        for c in range(side):
            turned = jnp.concatenate([gathered[b0, c1, :, c * feat : (c + 1) * feat] for c1 in range(side)], axis=1)
            x = jnp.concatenate([turned, gathered[b1, c]], axis=0)
            gate += lax.dot_general(x, gate_up[0, :, c * wide : (c + 1) * wide], contract, preferred_element_type=F32)
            up += lax.dot_general(x, gate_up[1, :, c * wide : (c + 1) * wide], contract, preferred_element_type=F32)
        hidden = (gate / (1.0 + jnp.exp(-gate)) * up).astype(BF16)
        for c0 in range(side):
            piece = jnp.dot(hidden, down[:, c0 * wide : (c0 + 1) * wide], preferred_element_type=F32).astype(BF16)
            part[b0, c0] = piece[:block_rows]
            for c1 in range(side):
                part[b1, c1, :, c0 * feat : (c0 + 1) * feat] = piece[block_rows:, c1 * feat : (c1 + 1) * feat]
        for b in (b0, b1):
            first = b % 2
            across = part.at[b, lax.rem(coords[first] + 2, side)]
            for way, o in enumerate((1, -1)):
                push(
                    across.at[:, pl.ds(way * mid, mid)], halves.at[b, way], rhalf_send, rhalf_recv.at[b, way],
                    (d, peer(first, o)),
                )

    def fold(b):
        first = b % 2
        for way, o in enumerate((1, -1)):
            await_bytes(halves.at[b, way], rhalf_recv.at[b, way])
            to = lax.rem(coords[first] + side + o, side)
            span = slice(way * mid, (way + 1) * mid)
            part[b, to, :, span] = (part[b, to, :, span].astype(F32) + halves[b, way].astype(F32)).astype(BF16)
            push(part.at[b, to], wholes.at[b, way], rwhole_send, rwhole_recv.at[b, way], (d, peer(first, o)))

    def narrow(b):
        first, second = b % 2, 1 - b % 2
        total = part[b, coords[first]].astype(F32)
        for way in range(2):
            await_bytes(wholes.at[b, way], rwhole_recv.at[b, way])
            total += wholes[b, way].astype(F32)
        for c in range(side):
            sums[b, c] = total[:, c * feat : (c + 1) * feat].astype(BF16)
        for o in range(1, side):
            push(
                sums.at[b, lax.rem(coords[second] + o, side)], landed.at[b, o - 1], last_send, last_recv.at[b],
                (d, peer(second, o)),
            )

    def finish(b):
        second = 1 - b % 2
        await_bytes(landed.at[b], last_recv.at[b])
        total = sums[b, coords[second]].astype(F32)
        for o in range(1, side):
            total += landed[b, o - 1].astype(F32)
        pairs = total.astype(BF16).reshape(block_rows // 2, 2, feat)
        results[pl.ds(b * block_rows // 2, block_rows // 2)] = pairs
        if b == 0:
            pltpu.make_async_copy(chunk(results, 0), chunk(returned, 0), own_sem).start()
        lax.fori_loop(max(1, b * per_block), (b + 1) * per_block, send2, 0)

    stages = (arrive, widen, forward, experts, fold, narrow, finish)
    order = sorted((pair * period + s, -s, pair) for pair in range(blocks // 2) for s in range(len(stages)))
    for _, s, pair in order:
        stage = stages[-s]
        if stage is experts:
            if pair == 0:
                for weight_load in weights:
                    weight_load.wait()
            experts(pair)
        else:
            stage(2 * pair)
            stage(2 * pair + 1)

    pltpu.make_async_copy(chunk(results, 0), chunk(returned, 0), own_sem).wait()
    await_bytes(returned.at[pl.ds(half, rows // 2 - half)], z2_recv)
    back = returned[...].reshape(rows, feat)
    total = jnp.zeros((tok, feat), F32)
    for i in range(3):
        total += lax.dot_general(terms[i], back, (((0,), (0,)), ((), ())), preferred_element_type=F32)
    out[...] = total.astype(BF16)

    await_bytes(outgoing.at[pl.ds(half, rows // 2 - half)], z1_send)
    await_bytes(results.at[pl.ds(half, rows // 2 - half)], z2_send)
    await_bytes(gathered.at[:, 0, :, pl.ds(0, wide - feat)], light_send)
    await_bytes(gathered.at[:, pl.ds(0, 2)], plane_send)
    await_bytes(gathered.at[:, 0], half_send)
    await_bytes(halves, rhalf_send)
    await_bytes(wholes, rwhole_send)
    await_bytes(landed, last_send)


def per_device(n, side, blocks, period, tokens, routes, gate_weights, gate_up_weight, down_weight):
    tok, feat = tokens.shape
    cap = 5 * tok // 64
    rows = n * cap
    block_rows = rows // blocks
    _, model, _, width = gate_up_weight.shape
    wide = side * feat
    gate_up = gate_up_weight.transpose(0, 2, 3, 1).reshape(2, width, model)
    down = down_weight.reshape(width, model)
    dma = pltpu.SemaphoreType.DMA
    anywhere = pl.BlockSpec(memory_space=pl.ANY)
    return pl.pallas_call(
        functools.partial(kernel, n, side, cap, blocks, period),
        out_shape=jax.ShapeDtypeStruct((tok, feat), BF16),
        in_specs=[anywhere] * 5,
        out_specs=pl.BlockSpec(memory_space=pltpu.VMEM),
        scratch_shapes=[
            pltpu.VMEM((tok, feat), BF16),
            pltpu.VMEM((routes.shape[1], tok), jnp.int32),
            pltpu.VMEM((routes.shape[1], tok), F32),
            pltpu.VMEM((2, width, model), BF16),
            pltpu.VMEM((width, model), BF16),
            pltpu.VMEM((3, rows, tok), BF16),
            pltpu.VMEM((rows // 2, 2, feat), BF16),
            pltpu.VMEM((rows // 2, 2, feat), BF16),
            pltpu.VMEM((blocks, side, block_rows, wide), BF16),
            pltpu.VMEM((blocks, side, block_rows, wide), BF16),
            pltpu.VMEM((blocks, 2, block_rows, wide // 2), BF16),
            pltpu.VMEM((blocks, 2, block_rows, wide), BF16),
            pltpu.VMEM((blocks, side, block_rows, feat), BF16),
            pltpu.VMEM((blocks, side - 1, block_rows, feat), BF16),
            pltpu.VMEM((rows // 2, 2, feat), BF16),
            pltpu.VMEM((rows // 2, 2, feat), BF16),
            dma((5,)),
            dma,
            dma,
            dma((blocks,)),
            dma,
            dma((blocks,)),
            dma,
            dma((blocks, 2)),
            dma,
            dma((blocks, 2)),
            dma,
            dma((blocks, 2)),
            dma,
            dma((blocks, 2)),
            dma,
            dma((blocks,)),
            dma,
            dma,
        ],
        compiler_params=pltpu.CompilerParams(
            collective_id=0, has_side_effects=True, vmem_limit_bytes=63_000_000
        ),
        cost_estimate=pl.CostEstimate(
            flops=6 * rows * model * width, bytes_accessed=6 * width * model, transcendentals=rows * width
        ),
    )(tokens, routes.T, gate_weights.T, gate_up, down)


def solution(mesh):
    n = mesh.shape["dp"]
    side = math.isqrt(mesh.shape["expert"])
    return jax.shard_map(
        functools.partial(per_device, n, side, BLOCKS, PERIOD),
        mesh=mesh,
        in_specs=(
            P("dp", "expert"),
            P("dp", None),
            P("dp", None),
            P("dp", None, None, "expert"),
            P("dp", "expert", None),
        ),
        out_specs=P("dp", "expert"),
        check_vma=False,
    )
```

time: 110 us -> 97.1 us (0.88)
  Pallas kernels: 104 us -> 95.5 us
  local copies, waits for them, and re-layouts: 5.21 us -> 1.38 us
    pallas_call x1, Pallas kernels: 104 us -> 95.5 us  [per_device(): pl.pallas_call(functools.partial(kernel, n, side, cap, blocks, period), o...]
    unnamed x11 -> x1, local copies, waits for them, and re-layouts: 5.21 us -> 1.38 us
where the time goes in v2:
time: 97.1 us; the launch traced here: 96.9 us
  Pallas kernels  95.5 us (98%)
  local copies, waits for them, and re-layouts  1.38 us (1%)
    pallas_call x1, Pallas kernels, per_device(): pl.pallas_call(functools.partial(kernel, n, side, cap, blocks, period), o...  95.5 us

profile of v2, /device:TPU:1, one launch (start us, length us, event | category | flops | bytes accessed | tf_op | source)
XLA Modules:
  0.0 96.9 jit_solution(18050619784536210989)
XLA Ops:
  0.0 95.5 %shard_map.55 = bf16[128,128]{1,0:T(8,128)(2,1)} custom-call(bf16[128,128]{1,0:T(8,128)(2,1)} %tokens_hbm.1, s32[4,128]{1,0:T(4,128)} %bitcast.8, f32[4,128]{1,0:T(4,128)} %bitcast.9, bf16[2,176,2048]{2,1,0:T(8,128)(2,1)} %bitcast.6, bf16[176,2048]{1,0:T(8,128)(2,1)} %bitcast.7), custom_call_target="tpu_custom_call" | custom-call | flops 1384120320 | bytes 2162688 | tf_op jit(solution)/shard_map/pallas_call | solution.py:264
  95.5 1.4 %copy.7 = bf16[128,128]{1,0:T(8,128)(2,1)} copy(bf16[128,128]{1,0:T(8,128)(2,1)} %shard_map.55) | data formatting | bytes 65536

commit v3 on v2

--- a/solution.py
+++ b/solution.py
@@ -89,6 +89,33 @@
     sent = jnp.dot(dispatch, tokens[...], preferred_element_type=F32).astype(BF16)
     outgoing[...] = sent.reshape(rows // 2, 2, feat)
 
+    pl.semaphore_wait(barrier, n - 1 + 2 * (side - 1))
+
+    def chunk(ref, i):
+        return ref.at[pl.ds(i * half, half)]
+
+    def push(src, dst, send, recv, to):
+        pltpu.make_async_remote_copy(
+            src, dst, send, recv, device_id=to, device_id_type=MESH_ID
+        ).start()
+
+    def await_bytes(ref, sem):
+        pltpu.make_async_copy(ref, ref, sem).wait()
+
+    def send1(i, carry):
+        to = (lax.rem(d - offset_of(i, n) + n, n), j)
+        push(chunk(outgoing, i), chunk(incoming, i), z1_send, z1_recv.at[i // per_block], to)
+        return carry
+
+    def send2(i, carry):
+        to = (lax.rem(d + offset_of(i, n), n), j)
+        push(chunk(results, i), chunk(returned, i), z2_send, z2_recv, to)
+        return carry
+
+    own = pltpu.make_async_copy(chunk(outgoing, 0), chunk(incoming, 0), own_sem)
+    own.start()
+    lax.fori_loop(1, min(n, 4 * per_block), send1, 0)
+
     load_gates.wait()
     weight = jnp.zeros((rows, tok), F32)
     for k, pick in enumerate(picks):
@@ -97,33 +124,6 @@
         term = weight.astype(BF16)
         weight = weight - term.astype(F32)
         terms[i] = term
-
-    pl.semaphore_wait(barrier, n - 1 + 2 * (side - 1))
-
-    def chunk(ref, i):
-        return ref.at[pl.ds(i * half, half)]
-
-    def push(src, dst, send, recv, to):
-        pltpu.make_async_remote_copy(
-            src, dst, send, recv, device_id=to, device_id_type=MESH_ID
-        ).start()
-
-    def await_bytes(ref, sem):
-        pltpu.make_async_copy(ref, ref, sem).wait()
-
-    def send1(i, carry):
-        to = (lax.rem(d - offset_of(i, n) + n, n), j)
-        push(chunk(outgoing, i), chunk(incoming, i), z1_send, z1_recv.at[i // per_block], to)
-        return carry
-
-    def send2(i, carry):
-        to = (lax.rem(d + offset_of(i, n), n), j)
-        push(chunk(results, i), chunk(returned, i), z2_send, z2_recv, to)
-        return carry
-
-    own = pltpu.make_async_copy(chunk(outgoing, 0), chunk(incoming, 0), own_sem)
-    own.start()
-    lax.fori_loop(1, n, send1, 0)
 
     def lanes(c, width):
         return pl.ds(pl.multiple_of(c * width, width), width)
@@ -231,6 +231,8 @@
         else:
             stage(2 * pair)
             stage(2 * pair + 1)
+            if stage is arrive and pair + 2 < blocks // 2:
+                lax.fori_loop((pair + 2) * 2 * per_block, (pair + 3) * 2 * per_block, send1, 0)
 
     pltpu.make_async_copy(chunk(results, 0), chunk(returned, 0), own_sem).wait()
     await_bytes(returned.at[pl.ds(half, rows // 2 - half)], z2_recv)

time: 97.1 us -> 96.5 us (level)
  no operation moved by 1% of the time
where the time goes in v3:
time: 96.5 us; the launch traced here: 96.3 us
  Pallas kernels  95 us (98%)
  local copies, waits for them, and re-layouts  1.38 us (1%)
    pallas_call x1, Pallas kernels, per_device(): pl.pallas_call(functools.partial(kernel, n, side, cap, blocks, period), o...  95 us

profile of v3, /device:TPU:1, one launch (start us, length us, event | category | flops | bytes accessed | tf_op | source)
XLA Modules:
  0.0 96.3 jit_solution(14113277848966766637)
XLA Ops:
  0.0 95.0 %shard_map.55 = bf16[128,128]{1,0:T(8,128)(2,1)} custom-call(bf16[128,128]{1,0:T(8,128)(2,1)} %tokens_hbm.1, s32[4,128]{1,0:T(4,128)} %bitcast.8, f32[4,128]{1,0:T(4,128)} %bitcast.9, bf16[2,176,2048]{2,1,0:T(8,128)(2,1)} %bitcast.6, bf16[176,2048]{1,0:T(8,128)(2,1)} %bitcast.7), custom_call_target="tpu_custom_call" | custom-call | flops 1384120320 | bytes 2162688 | tf_op jit(solution)/shard_map/pallas_call | solution.py:266
  95.0 1.4 %copy.7 = bf16[128,128]{1,0:T(8,128)(2,1)} copy(bf16[128,128]{1,0:T(8,128)(2,1)} %shard_map.55) | data formatting | bytes 65536
